TPU v7x, 32 devices: a whole 2x2x4 slice. The times are simulated.
32 devices in a mesh: dp: 8 (over z, core), land: 4 (over y, x).
Axes of the slice: x: 2, y: 2, z: 4, core: 2. Of those that a mesh axis runs over, the one named last changes fastest.
Arguments:
- doc_values: bfloat16 [12288, 1024], P('dp'), may hold values from 0 to 100
- doc_blocks: int32 [96, 8], P('dp'), may hold values from 0 to 511, as said below
- land_values: bfloat16 [16384, 1024], P(('dp', 'land')), may hold values from 0 to 100
- land_blocks: int32 [128, 8], replicated, may hold values from 0 to 511, as said below
- coefficients: bfloat16 [16384, 64], P(('dp', 'land')), may hold values from -12 to 12
Outputs:
- normal_product: float32 [16384, 64], P(('dp', 'land'))
Inputs may be any that keep to these rules, and one draw needn't show every extreme that they name: `doc_blocks`: each row lists 8 different vocabulary block numbers. `land_blocks`: each row lists 8 different vocabulary block numbers.
All inputs are finite; a program needn't handle non-finite values.
Results may differ from a plain program's by a relative error of at most 0.0003.
Values may be sent and summed in bfloat16 or wider, within the bound.
A program may use at most 128 MiB of HBM per device.

v0:
```python
import jax
import jax.numpy as jnp
from jax import lax
from jax.sharding import PartitionSpec as P

TERM_BLOCK = 128
ACTIVE = 8
LAND_ACTIVE = 8
DOC_BLOCK = 128
LM_BLOCK = 128


sharpness = 2.0


def split_pair(values):
    high = lax.optimization_barrier(values.astype(jnp.bfloat16))
    low = (values - high.astype(jnp.float32)).astype(jnp.bfloat16)
    return (high, low)


def kernel_tiles(doc_grid, doc_blocks, doc_norm, land_rows, land_ids):
    block_count = land_ids.shape[0]
    land_norm = lax.rsqrt(jnp.sum(jnp.square(land_rows.astype(jnp.float32)), axis=1) + 1e-06)
    land_grid = land_rows.reshape(block_count, LM_BLOCK, LAND_ACTIVE, TERM_BLOCK)
    norm_grid = land_norm.reshape(block_count, LM_BLOCK)

    def one_block(packed):
        tile_grid, tile_ids, tile_norms = packed
        matches = (doc_blocks[:, :, None] == tile_ids[None, None, :]).astype(jnp.bfloat16)
        aligned = jnp.einsum(
            "dab,lbt->dlat", matches, tile_grid, preferred_element_type=jnp.float32
        ).astype(jnp.bfloat16)
        aligned = aligned.reshape(matches.shape[0], LM_BLOCK, ACTIVE * TERM_BLOCK)
        inner_terms = jnp.einsum(
            "drw,dlw->drl", doc_grid, aligned, preferred_element_type=jnp.float32
        )
        inner_terms = inner_terms.reshape(-1, LM_BLOCK)
        cosine = inner_terms * doc_norm[:, None] * tile_norms[None, :]
        return split_pair(jnp.exp(2.0 * sharpness * (cosine - 1.0)))

    return lax.map(one_block, (land_grid, land_ids, norm_grid))


def on_device(doc_values, doc_blocks, land_values, land_blocks, coefficients):
    dp_count = lax.axis_size("dp")
    land_count = lax.axis_size("land")
    doc_rows = doc_values.shape[0]
    targets = coefficients.shape[1]
    total_docs = doc_rows * dp_count
    own_blocks = land_values.shape[0] // LM_BLOCK
    doc_norm = lax.rsqrt(jnp.sum(jnp.square(doc_values.astype(jnp.float32)), axis=1) + 1e-06)
    doc_grid = doc_values.reshape(doc_rows // DOC_BLOCK, DOC_BLOCK, ACTIVE * TERM_BLOCK)
    table = land_blocks.reshape(dp_count, land_count, own_blocks, LAND_ACTIVE)
    own_table = lax.dynamic_index_in_dim(table, lax.axis_index("land"), axis=1, keepdims=False)
    own_table = own_table.reshape(dp_count * own_blocks, LAND_ACTIVE)
    land_rows = lax.all_gather(land_values, "dp", axis=0, tiled=True)
    coef_rows = lax.all_gather(coefficients, "dp", axis=0, tiled=True)
    tile_high, tile_low = kernel_tiles(doc_grid, doc_blocks, doc_norm, land_rows, own_table)
    coef_grid = coef_rows.reshape(tile_high.shape[0], LM_BLOCK, -1)
    part_one = jnp.einsum("qnl,qlt->nt", tile_high, coef_grid, preferred_element_type=jnp.float32)
    fitted = part_one + jnp.einsum(
        "qnl,qlt->nt", tile_low, coef_grid, preferred_element_type=jnp.float32
    )
    absorb_high_all = tile_high
    absorb_low_all = tile_low
    folded = (fitted, absorb_high_all, absorb_low_all)
    fitted = folded[0]
    fitted = lax.psum(fitted, "land")
    fitted_high, fitted_low = split_pair(fitted)
    fitted_pair = jnp.concatenate([fitted_high, fitted_low], axis=1)
    high_all = folded[1]
    low_all = folded[2]
    tile_high = high_all
    tile_low = low_all
    summed = jnp.einsum("qnl,nt->qlt", tile_high, fitted_pair, preferred_element_type=jnp.float32)
    summed = summed + jnp.einsum(
        "qnl,nt->qlt", tile_low, fitted_pair, preferred_element_type=jnp.float32
    )
    summed = summed[:, :, :targets] + summed[:, :, targets:]
    result = lax.psum_scatter(summed.reshape(-1, targets), "dp", scatter_dimension=0, tiled=True)
    return result / total_docs


def solution(mesh):
    placed = (P("dp", None), P("dp", None), P(("dp", "land"), None), P(), P(("dp", "land"), None))
    return jax.shard_map(
        on_device, mesh=mesh, in_specs=placed, out_specs=P(("dp", "land"), None), check_vma=False
    )
```

profile of v0, /device:TPU:0, one launch (start us, length us, event | category | flops | bytes accessed | tf_op | source)
XLA Modules:
  0.0 750.0 jit_solution(13663810551851997529)
XLA Ops:
  10.7 19.0 %all_gather.7 = bf16[4096,64]{0,1:T(8,128)(2,1)} all-gather(bf16[512,64]{0,1:T(8,128)(2,1)} %param.11), channel_id=1, replica_groups=mesh['dp'=8,'land'=4] {'dp'}, dimensions={0}, use_global_device_ids=true | all-gather | bytes 589824 | tf_op jit(solution)/shard_map/all_gather | solution.py:58
  29.7 65.4 %all-gather.2.cloned.1.call-done = bf16[4096,1024]{1,0:T(8,128)(2,1)} async-done(((bf16[512,1024]{1,0:T(8,128)(2,1)}), bf16[4096,1024]{1,0:T(8,128)(2,1)}) %all-gather.2.cloned.1.call-update) | async-done | bytes 8388624 | tf_op jit(solution)/shard_map/all_gather | solution.py:57
  95.1 8.8 %copy.17 = bf16[512,8,8,128]{3,2,1,0:T(8,128)(2,1)} copy(bf16[512,8,8,128]{3,1,2,0:T(8,128)(2,1)} %bitcast.99) | data formatting | bytes 16777216
  109.0 527.9 %while.14 = (s32[]{:T(128)}, bf16[32,1536,128]{2,1,0:T(8,128)(2,1)}, bf16[32,1536,128]{2,1,0:T(8,128)(2,1)}, bf16[32,128,8,128]{3,2,1,0:T(8,128)(2,1)}, s32[12,8...) while((s32[]{:T(128)}, ...), condition=%wide.region_3.4_spmd, body=%wide.region_2.3_spmd.sunk | while | flops 431751936 | bytes 19938892 | solution.py:42
  113.4 7.8 %copy.28 = bf16[12,128,8,128]{1,3,2,0:T(8,128)(2,1)S(1)} copy(bf16[12,128,8,128]{3,0,2,1:T(8,128)(2,1)} %convert_bitcast_fusion.2) | data formatting | bytes 6291456 | tf_op jit(solution)/shard_map/while/body/eval_jaxpr/convert_element_type | solution.py:33
  129.9 7.8 %copy.28 = bf16[12,128,8,128]{1,3,2,0:T(8,128)(2,1)S(1)} copy(bf16[12,128,8,128]{3,0,2,1:T(8,128)(2,1)} %convert_bitcast_fusion.2) | data formatting | bytes 6291456 | tf_op jit(solution)/shard_map/while/body/eval_jaxpr/convert_element_type | solution.py:33
  146.4 7.8 %copy.28 = bf16[12,128,8,128]{1,3,2,0:T(8,128)(2,1)S(1)} copy(bf16[12,128,8,128]{3,0,2,1:T(8,128)(2,1)} %convert_bitcast_fusion.2) | data formatting | bytes 6291456 | tf_op jit(solution)/shard_map/while/body/eval_jaxpr/convert_element_type | solution.py:33
  162.9 7.8 %copy.28 = bf16[12,128,8,128]{1,3,2,0:T(8,128)(2,1)S(1)} copy(bf16[12,128,8,128]{3,0,2,1:T(8,128)(2,1)} %convert_bitcast_fusion.2) | data formatting | bytes 6291456 | tf_op jit(solution)/shard_map/while/body/eval_jaxpr/convert_element_type | solution.py:33
  179.5 7.8 %copy.28 = bf16[12,128,8,128]{1,3,2,0:T(8,128)(2,1)S(1)} copy(bf16[12,128,8,128]{3,0,2,1:T(8,128)(2,1)} %convert_bitcast_fusion.2) | data formatting | bytes 6291456 | tf_op jit(solution)/shard_map/while/body/eval_jaxpr/convert_element_type | solution.py:33
  196.0 7.8 %copy.28 = bf16[12,128,8,128]{1,3,2,0:T(8,128)(2,1)S(1)} copy(bf16[12,128,8,128]{3,0,2,1:T(8,128)(2,1)} %convert_bitcast_fusion.2) | data formatting | bytes 6291456 | tf_op jit(solution)/shard_map/while/body/eval_jaxpr/convert_element_type | solution.py:33
  212.5 7.8 %copy.28 = bf16[12,128,8,128]{1,3,2,0:T(8,128)(2,1)S(1)} copy(bf16[12,128,8,128]{3,0,2,1:T(8,128)(2,1)} %convert_bitcast_fusion.2) | data formatting | bytes 6291456 | tf_op jit(solution)/shard_map/while/body/eval_jaxpr/convert_element_type | solution.py:33
  229.0 7.8 %copy.28 = bf16[12,128,8,128]{1,3,2,0:T(8,128)(2,1)S(1)} copy(bf16[12,128,8,128]{3,0,2,1:T(8,128)(2,1)} %convert_bitcast_fusion.2) | data formatting | bytes 6291456 | tf_op jit(solution)/shard_map/while/body/eval_jaxpr/convert_element_type | solution.py:33
  245.5 7.8 %copy.28 = bf16[12,128,8,128]{1,3,2,0:T(8,128)(2,1)S(1)} copy(bf16[12,128,8,128]{3,0,2,1:T(8,128)(2,1)} %convert_bitcast_fusion.2) | data formatting | bytes 6291456 | tf_op jit(solution)/shard_map/while/body/eval_jaxpr/convert_element_type | solution.py:33
  295.0 7.8 %copy.28 = bf16[12,128,8,128]{1,3,2,0:T(8,128)(2,1)S(1)} copy(bf16[12,128,8,128]{3,0,2,1:T(8,128)(2,1)} %convert_bitcast_fusion.2) | data formatting | bytes 6291456 | tf_op jit(solution)/shard_map/while/body/eval_jaxpr/convert_element_type | solution.py:33
  311.4 7.8 %copy.28 = bf16[12,128,8,128]{1,3,2,0:T(8,128)(2,1)S(1)} copy(bf16[12,128,8,128]{3,0,2,1:T(8,128)(2,1)} %convert_bitcast_fusion.2) | data formatting | bytes 6291456 | tf_op jit(solution)/shard_map/while/body/eval_jaxpr/convert_element_type | solution.py:33
  393.8 7.8 %copy.28 = bf16[12,128,8,128]{1,3,2,0:T(8,128)(2,1)S(1)} copy(bf16[12,128,8,128]{3,0,2,1:T(8,128)(2,1)} %convert_bitcast_fusion.2) | data formatting | bytes 6291456 | tf_op jit(solution)/shard_map/while/body/eval_jaxpr/convert_element_type | solution.py:33
  410.3 7.8 %copy.28 = bf16[12,128,8,128]{1,3,2,0:T(8,128)(2,1)S(1)} copy(bf16[12,128,8,128]{3,0,2,1:T(8,128)(2,1)} %convert_bitcast_fusion.2) | data formatting | bytes 6291456 | tf_op jit(solution)/shard_map/while/body/eval_jaxpr/convert_element_type | solution.py:33
  476.2 7.8 %copy.28 = bf16[12,128,8,128]{1,3,2,0:T(8,128)(2,1)S(1)} copy(bf16[12,128,8,128]{3,0,2,1:T(8,128)(2,1)} %convert_bitcast_fusion.2) | data formatting | bytes 6291456 | tf_op jit(solution)/shard_map/while/body/eval_jaxpr/convert_element_type | solution.py:33
  509.2 7.8 %copy.28 = bf16[12,128,8,128]{1,3,2,0:T(8,128)(2,1)S(1)} copy(bf16[12,128,8,128]{3,0,2,1:T(8,128)(2,1)} %convert_bitcast_fusion.2) | data formatting | bytes 6291456 | tf_op jit(solution)/shard_map/while/body/eval_jaxpr/convert_element_type | solution.py:33
  608.3 7.8 %copy.28 = bf16[12,128,8,128]{1,3,2,0:T(8,128)(2,1)S(1)} copy(bf16[12,128,8,128]{3,0,2,1:T(8,128)(2,1)} %convert_bitcast_fusion.2) | data formatting | bytes 6291456 | tf_op jit(solution)/shard_map/while/body/eval_jaxpr/convert_element_type | solution.py:33
  624.8 7.8 %copy.28 = bf16[12,128,8,128]{1,3,2,0:T(8,128)(2,1)S(1)} copy(bf16[12,128,8,128]{3,0,2,1:T(8,128)(2,1)} %convert_bitcast_fusion.2) | data formatting | bytes 6291456 | tf_op jit(solution)/shard_map/while/body/eval_jaxpr/convert_element_type | solution.py:33
  636.9 8.6 %convolution_bitcast_fusion = f32[1536,64]{0,1:T(8,128)S(1)} fusion(bf16[32,1536,128]{2,1,0:T(8,128)(2,1)} %get-tuple-element.120, bf16[4096,64]{0,1:T(8,128)(2,1)} %all_gather.7), kind=kOutput, calls=%fused_computation.23 | convolution fusion | flops 805306368 | bytes 13500416 | tf_op jit(solution)/shard_map/qnl,qlt->nt/dot_general | solution.py:62
  650.5 42.8 %all-reduce.2.cloned.1.call-done = f32[1536,64]{0,1:T(8,128)} async-done(((f32[1536,64]{0,1:T(8,128)}), f32[1536,64]{0,1:T(8,128)}) %all-reduce.2.cloned.1.call-update) | async-done | bytes 393232 | tf_op jit(solution)/shard_map/psum | solution.py:69
  709.5 32.4 %reduce-scatter.2.cloned.1.call-done = f32[512,64]{0,1:T(8,128)} async-done(((f32[4096,64]{0,1:T(8,128)}), f32[512,64]{0,1:T(8,128)}) %reduce-scatter.2.cloned.1.call-update) | async-done | bytes 131088 | tf_op jit(solution)/shard_map/reduce_scatter | solution.py:81
  (234 shorter events, 426.9 us)
Async XLA Ops:
  6.5 88.6 %all-gather.2.cloned.1.call-start = ((), (), s32[]{:S(2)}) async-start(), calls=%async_computation.1 | async-start | bytes 9437184 | tf_op jit(solution)/shard_map/all_gather | solution.py:57
  7.3 686.1 %all-reduce.2.cloned.1.call-start = ((), (), s32[]{:S(2)}) async-start(), calls=%async_computation.2 | async-start | bytes 786432 | tf_op jit(solution)/shard_map/psum | solution.py:69
  95.1 13.9 %copy-start.2 = (s32[12,8]{0,1:T(8,128)S(1)}, s32[12,8]{0,1:T(8,128)}, u32[]{:S(2)}) copy-start(s32[12,8]{0,1:T(8,128)} %param.8) | copy-start | bytes 1156
  636.9 8.7 %copy-start = (bf16[32,1536,128]{2,1,0:T(8,128)(2,1)S(1)}, bf16[32,1536,128]{2,1,0:T(8,128)(2,1)}, u32[]{:S(2)}) copy-start(bf16[32,1536,128]{2,1,0:T(8,128)(2,1)} %get-tuple-element.119) | copy-start | bytes 37748740
  636.9 8.7 %copy-start.1 = (bf16[4096,64]{0,1:T(8,128)(2,1)S(1)}, bf16[4096,64]{0,1:T(8,128)(2,1)}, u32[]{:S(2)}) copy-start(bf16[4096,64]{0,1:T(8,128)(2,1)} %all_gather.7) | copy-start | bytes 1572868
  650.3 91.6 %reduce-scatter.2.cloned.1.call-start = ((), (), s32[]{:S(2)}) async-start(), calls=%async_computation.3 | async-start | bytes 1179648 | tf_op jit(solution)/shard_map/reduce_scatter | solution.py:81
Sparse Core Ops, SparseCore 0:
  9.0 86.1 all-gather.1
  650.4 42.8 all-reduce.1
  709.6 32.2 reduce-scatter.1
where the time goes:
time: 755 us; the launch traced here: 750 us
  local copies, waits for them, and re-layouts  258 us (34%)
  matrix products  257 us (34%)
  waiting for transfers between devices  141 us (19%)
  other arithmetic  59.6 us (8%)
  blocking collectives  19 us (3%)
  between operations  13.2 us (2%)
    convert_element_type x32, local copies, waits for them, and re-layouts, one_block(): aligned = jnp.einsum('dab,lbt->dlat', matches, tile_grid, preferred_eleme...  248 us
    dot_general x32, matrix products, one_block(): jnp.einsum('dab,lbt->dlat', matches, tile_grid, preferred_element_type=jn...  139 us
    dot_general x32, matrix products, one_block(): jnp.einsum('drw,dlw->drl', doc_grid, aligned, preferred_element_type=jnp....  91.5 us
    all_gather x1, waiting for transfers between devices, on_device(): land_rows = lax.all_gather(land_values, 'dp', axis=0, tiled=True)  65.4 us
    psum x1, waiting for transfers between devices, on_device(): fitted = lax.psum(fitted, 'land')  42.8 us
    dynamic_update_slice x32, other arithmetic, kernel_tiles(): return lax.map(one_block, (land_grid, land_ids, norm_grid))  38.2 us
    reduce_scatter x1, waiting for transfers between devices, on_device(): lax.psum_scatter(summed.reshape(-1, targets), 'dp', scatter_dimension=0,...  32.4 us
    all_gather x1, blocking collectives, on_device(): coef_rows = lax.all_gather(coefficients, 'dp', axis=0, tiled=True)  19 us
  transfers between devices with their start and end apart: 3, of which 3 were waited for; matrix products, arithmetic and copies ran while one was open for 0% of the time, Pallas kernels for 0%

commit v1 on v0

v1 whole, which is shorter than its diff:
```python
import functools
import jax
import jax.numpy as jnp
from jax import lax
from jax.experimental import pallas as pl
from jax.experimental.pallas import tpu as pltpu
from jax.sharding import PartitionSpec as P

TERM_BLOCK = 128
ACTIVE = 8
LAND_ACTIVE = 8
DOC_BLOCK = 128
LM_BLOCK = 128
SHARPNESS = 2.0
LOG2E = 1.4426950408889634
EPS = 1e-06
MESH = pl.DeviceIdType.MESH


def row_squares(rows):
    wide = rows.astype(jnp.float32)
    return jnp.sum(wide * wide, axis=1, keepdims=True)


def fused_kernel(
    dp_count, land_count, total_docs,
    pos_ref, doc_ref, land_ref, coef_ref, out_ref,
    lbuf, cbuf, work, kh, kl, dnorm, fit, fpart, full, fpair, sbuf, pbuf, rbuf,
    local_sem, own_send, own_csend, fz_send, fp_send, cfz_send, cfp_send, lrecv, crecv,
    f1_send, f1_recv, f2_send, f2_recv, p_send, p_recv, r_send, r_recv,
):
    nz = dp_count // 2
    nb = land_ref.shape[0]
    nd = doc_ref.shape[0]
    docs = nd * DOC_BLOCK
    targets = coef_ref.shape[0]
    part_rows = targets // land_count
    me = lax.axis_index("dp")
    ml = lax.axis_index("land")
    z = me // 2
    core = me % 2
    mate = z * 2 + (1 - core)

    barrier = pltpu.get_barrier_semaphore()
    pl.semaphore_signal(barrier, inc=1, device_id=(mate, ml), device_id_type=MESH)
    for off in range(1, nz):
        other = lax.rem(z + off, nz) * 2 + core
        pl.semaphore_signal(barrier, inc=1, device_id=(other, ml), device_id_type=MESH)
    for off in range(1, land_count):
        other = lax.rem(ml + off, land_count)
        pl.semaphore_signal(barrier, inc=1, device_id=(me, other), device_id_type=MESH)
    pl.semaphore_wait(barrier, 1 + (nz - 1) + (land_count - 1))

    def own_copy(b, way, device):
        return pltpu.make_async_remote_copy(
            src_ref=land_ref.at[b], dst_ref=lbuf.at[me, b],
            send_sem=own_send.at[way, b], recv_sem=lrecv.at[me, b],
            device_id=(device, ml), device_id_type=MESH)

    def own_coef(way, device):
        return pltpu.make_async_remote_copy(
            src_ref=coef_ref, dst_ref=cbuf.at[me],
            send_sem=own_csend.at[way], recv_sem=crecv.at[me],
            device_id=(device, ml), device_id_type=MESH)

    def forward(slot, b, send, device):
        return pltpu.make_async_remote_copy(
            src_ref=lbuf.at[slot, b], dst_ref=lbuf.at[slot, b],
            send_sem=send, recv_sem=lrecv.at[slot, b],
            device_id=(device, ml), device_id_type=MESH)

    def forward_coef(slot, send, device):
        return pltpu.make_async_remote_copy(
            src_ref=cbuf.at[slot], dst_ref=cbuf.at[slot],
            send_sem=send, recv_sem=crecv.at[slot],
            device_id=(device, ml), device_id_type=MESH)

    ways = ((0, z > 0, me - 2), (1, z < nz - 1, me + 2))

    def start_own(b, carry):
        for way, there, device in ways:
            @pl.when(there)
            def _():
                @pl.when(b == 0)
                def _():
                    own_coef(way, device).start()
                own_copy(b, way, device).start()

        @pl.when(b == 0)
        def _():
            own_coef(2, mate).start()
        own_copy(b, 2, mate).start()
        return carry

    lax.fori_loop(0, nb, start_own, 0)
    keep_land = pltpu.make_async_copy(land_ref, lbuf.at[me], local_sem.at[0])
    keep_coef = pltpu.make_async_copy(coef_ref, cbuf.at[me], local_sem.at[1])
    keep_land.start()
    keep_coef.start()

    work[LAND_ACTIVE] = jnp.zeros((2 * LM_BLOCK, TERM_BLOCK), jnp.bfloat16)
    fit[...] = jnp.zeros_like(fit)

    def doc_norms(d, carry):
        scale = (2.0 * SHARPNESS * LOG2E) * lax.rsqrt(row_squares(doc_ref[d]) + EPS)
        dnorm[d] = jnp.transpose(jnp.broadcast_to(scale, (DOC_BLOCK, DOC_BLOCK)))[0:8, :]
        return carry

    lax.fori_loop(0, nd, doc_norms, 0)
    keep_land.wait()
    keep_coef.wait()

    def compute(q, b):
        norms = []
        for c in range(2):
            for a in range(LAND_ACTIVE):
                work[a, c * LM_BLOCK:(c + 1) * LM_BLOCK, :] = (
                    lbuf[q * 2 + c, b, :, a * TERM_BLOCK:(a + 1) * TERM_BLOCK])
            norms.append(lax.rsqrt(row_squares(lbuf[q * 2 + c, b]) + EPS))
        norm = jnp.concatenate(norms, axis=0)
        start = pl.multiple_of(b * LM_BLOCK, LM_BLOCK)
        coef = jnp.concatenate(
            [cbuf[q * 2, :, pl.ds(start, LM_BLOCK)], cbuf[q * 2 + 1, :, pl.ds(start, LM_BLOCK)]],
            axis=1)
        unit = q * nb + b

        def doc_pair(i, carry):
            highs, lows = [], []
            for h in range(2):
                d = i * 2 + h
                sides = []
                for c in range(2):
                    first = (((q * 2 + c) * nb + b) * nd + d) * ACTIVE
                    sides.append(jnp.concatenate(
                        [work[pos_ref[first + a], c * LM_BLOCK:(c + 1) * LM_BLOCK, :]
                         for a in range(ACTIVE)], axis=1))
                aligned = jnp.concatenate(sides, axis=0)
                inner = lax.dot_general(
                    aligned, doc_ref[d], (((1,), (1,)), ((), ())),
                    preferred_element_type=jnp.float32)
                power = inner * norm * dnorm[d][0:1, :] - (2.0 * SHARPNESS * LOG2E)
                kernel = jnp.exp2(power)
                high = kernel.astype(jnp.bfloat16)
                highs.append(high)
                lows.append((kernel - high.astype(jnp.float32)).astype(jnp.bfloat16))
            high = jnp.concatenate(highs, axis=1)
            low = jnp.concatenate(lows, axis=1)
            cols = pl.ds(pl.multiple_of(i * 2 * DOC_BLOCK, 2 * DOC_BLOCK), 2 * DOC_BLOCK)
            kh[unit, :, cols] = high
            kl[unit, :, cols] = low
            fit[:, cols] += (
                jnp.dot(coef, high, preferred_element_type=jnp.float32)
                + jnp.dot(coef, low, preferred_element_type=jnp.float32))
            return carry

        lax.fori_loop(0, nd // 2, doc_pair, 0)

    def place(r, way):
        hops = r // nb
        q = z + hops * (2 * way - 1)
        return q, r % nb, (q >= 0) & (q < nz)

    def rounds(r, carry):
        for way, there, device in ways:
            @pl.when(r >= nb)
            def _():
                q, b, valid = place(r, way)
                onward = z + (1 - 2 * way)

                @pl.when(valid)
                def _():
                    slot = q * 2 + core
                    forward(slot, b, fp_send.at[q, b], mate).wait_recv()
                    @pl.when((onward >= 0) & (onward < nz))
                    def _():
                        forward(slot, b, fz_send.at[q, b], onward * 2 + core).start()
                    forward(slot, b, fp_send.at[q, b], mate).start()
                    @pl.when(b == 0)
                    def _():
                        forward_coef(slot, cfp_send.at[q], mate).wait_recv()
                        @pl.when((onward >= 0) & (onward < nz))
                        def _():
                            forward_coef(slot, cfz_send.at[q], onward * 2 + core).start()
                        forward_coef(slot, cfp_send.at[q], mate).start()

        def one_way(way, inner_carry):
            q, b, valid = place(r, way)

            @pl.when(valid & ((r >= nb) | (way == 0)))
            def _():
                slot = q * 2 + 1 - core
                forward(slot, b, fp_send.at[q, b], mate).wait_recv()
                @pl.when(b == 0)
                def _():
                    forward_coef(slot, cfp_send.at[q], mate).wait_recv()
                compute(q, b)
            return inner_carry

        lax.fori_loop(0, 2, one_way, 0)
        return carry

    lax.fori_loop(0, nz * nb, rounds, 0)

    def fit_out(off):
        peer = lax.rem(ml + off, land_count)
        rows = pl.ds(pl.multiple_of(peer * part_rows, part_rows), part_rows)
        return pltpu.make_async_remote_copy(
            src_ref=fit.at[rows], dst_ref=fpart.at[ml],
            send_sem=f1_send.at[off], recv_sem=f1_recv.at[ml],
            device_id=(me, peer), device_id_type=MESH)

    def fit_in(off):
        peer = lax.rem(ml + off, land_count)
        rows = pl.ds(pl.multiple_of(ml * part_rows, part_rows), part_rows)
        return pltpu.make_async_remote_copy(
            src_ref=fit.at[rows], dst_ref=fpart.at[peer],
            send_sem=f1_send.at[off], recv_sem=f1_recv.at[peer],
            device_id=(me, peer), device_id_type=MESH)

    def full_copy(owner, off, sem_slot):
        peer = lax.rem(ml + off, land_count)
        rows = pl.ds(pl.multiple_of(owner * part_rows, part_rows), part_rows)
        return pltpu.make_async_remote_copy(
            src_ref=full.at[rows], dst_ref=full.at[rows],
            send_sem=f2_send.at[off], recv_sem=f2_recv.at[sem_slot],
            device_id=(me, peer), device_id_type=MESH)

    for off in range(1, land_count):
        fit_out(off).start()
    mine = pl.ds(pl.multiple_of(ml * part_rows, part_rows), part_rows)
    total = fit[mine, :]
    for off in range(1, land_count):
        fit_in(off).wait_recv()
        total = total + fpart[lax.rem(ml + off, land_count)]
    full[mine, :] = total
    for off in range(1, land_count):
        full_copy(ml, off, ml).start()
    for off in range(1, land_count):
        peer = lax.rem(ml + off, land_count)
        full_copy(peer, off, peer).wait_recv()
    fitted = full[...]
    fitted_high = fitted.astype(jnp.bfloat16)
    fpair[0:targets, :] = fitted_high
    fpair[targets:, :] = (fitted - fitted_high.astype(jnp.float32)).astype(jnp.bfloat16)

    half = LM_BLOCK // 2
    lane = lax.broadcasted_iota(jnp.int32, (half, 2 * targets), 1)

    def mate_copy(q):
        return pltpu.make_async_remote_copy(
            src_ref=sbuf.at[1 - core, q], dst_ref=pbuf.at[q],
            send_sem=p_send.at[q], recv_sem=p_recv.at[q],
            device_id=(mate, ml), device_id_type=MESH)

    def chip_copy(q, source):
        return pltpu.make_async_remote_copy(
            src_ref=sbuf.at[core, q], dst_ref=rbuf.at[source],
            send_sem=r_send.at[q], recv_sem=r_recv.at[source],
            device_id=(q * 2 + core, ml), device_id_type=MESH)

    def finish(q):
        mate_copy(q).wait_recv()
        sbuf[core, q] = sbuf[core, q] + pbuf[q]

    def back(i, carry):
        q = lax.rem(z + 1 + i, nz)

        def back_unit(b, inner_carry):
            unit = q * nb + b
            pair = fpair[...]
            dims = (((1,), (1,)), ((), ()))
            summed = (
                lax.dot_general(kh[unit], pair, dims, preferred_element_type=jnp.float32)
                + lax.dot_general(kl[unit], pair, dims, preferred_element_type=jnp.float32))
            summed = summed + pltpu.roll(summed, targets, 1)
            at = pl.ds(pl.multiple_of(b * half, half), half)
            for c in range(2):
                low = c * LM_BLOCK
                sbuf[c, q, at, :] = jnp.where(
                    lane < targets, summed[low:low + half], summed[low + half:low + LM_BLOCK])
            return inner_carry

        lax.fori_loop(0, nb, back_unit, 0)
        mate_copy(q).start()

        @pl.when(i > 0)
        def _():
            before = lax.rem(z + i, nz)
            finish(before)
            chip_copy(before, z).start()
        return carry

    lax.fori_loop(0, nz, back, 0)
    finish(z)
    result = sbuf[core, z]
    for off in range(1, nz):
        source = lax.rem(z + off, nz)
        chip_copy(source, source).wait_recv()
        result = result + rbuf[source]
    result = result / total_docs
    for b in range(nb):
        piece = result[b * half:(b + 1) * half]
        out_ref[b * LM_BLOCK:b * LM_BLOCK + half, :] = piece[:, :targets]
        out_ref[b * LM_BLOCK + half:(b + 1) * LM_BLOCK, :] = piece[:, targets:]

    def end_own(b, carry):
        for way, there, device in ways:
            @pl.when(there)
            def _():
                own_copy(b, way, device).wait_send()
        own_copy(b, 2, mate).wait_send()
        return carry

    lax.fori_loop(0, nb, end_own, 0)
    for way, there, device in ways:
        @pl.when(there)
        def _():
            own_coef(way, device).wait_send()
    own_coef(2, mate).wait_send()

    def end_rounds(r, carry):
        for way, there, device in ways:
            q, b, valid = place(r, way)
            onward = z + (1 - 2 * way)

            @pl.when(valid)
            def _():
                slot = q * 2 + core
                on = (onward >= 0) & (onward < nz)
                @pl.when(on)
                def _():
                    forward(slot, b, fz_send.at[q, b], onward * 2 + core).wait_send()
                forward(slot, b, fp_send.at[q, b], mate).wait_send()
                @pl.when(b == 0)
                def _():
                    @pl.when(on)
                    def _():
                        forward_coef(slot, cfz_send.at[q], onward * 2 + core).wait_send()
                    forward_coef(slot, cfp_send.at[q], mate).wait_send()
        return carry

    lax.fori_loop(nb, nz * nb, end_rounds, 0)
    for off in range(1, land_count):
        fit_out(off).wait_send()
        full_copy(ml, off, ml).wait_send()
    for off in range(nz):
        mate_copy(lax.rem(z + off, nz)).wait_send()
    for off in range(1, nz):
        chip_copy(lax.rem(z + off, nz), z).wait_send()


def on_device(doc_values, doc_blocks, land_values, land_blocks, coefficients):
    dp_count = lax.axis_size("dp")
    land_count = lax.axis_size("land")
    docs = doc_values.shape[0]
    own = land_values.shape[0]
    targets = coefficients.shape[1]
    width = ACTIVE * TERM_BLOCK
    nz, nb, nd = dp_count // 2, own // LM_BLOCK, docs // DOC_BLOCK
    table = land_blocks.reshape(dp_count, land_count, nb, LAND_ACTIVE)
    table = lax.dynamic_index_in_dim(table, lax.axis_index("land"), axis=1, keepdims=False)
    table = table.reshape(dp_count * nb, LAND_ACTIVE)
    same = doc_blocks[None, :, :, None] == table[:, None, None, :]
    spots = jnp.where(same, jnp.arange(LAND_ACTIVE, dtype=jnp.int32), LAND_ACTIVE)
    pos = jnp.min(spots, axis=3).reshape(-1)
    dma = pltpu.SemaphoreType.DMA
    vmem = pl.BlockSpec(memory_space=pltpu.VMEM)
    units = nz * nb
    pairs = docs * dp_count * own
    half = own // 2
    return pl.pallas_call(
        functools.partial(fused_kernel, dp_count, land_count, float(docs * dp_count)),
        out_shape=jax.ShapeDtypeStruct((own, targets), jnp.float32),
        in_specs=[pl.BlockSpec(memory_space=pltpu.SMEM), vmem, vmem, vmem],
        out_specs=vmem,
        scratch_shapes=[
            pltpu.VMEM((dp_count, nb, LM_BLOCK, width), jnp.bfloat16),
            pltpu.VMEM((dp_count, targets, own), jnp.bfloat16),
            pltpu.VMEM((LAND_ACTIVE + 1, 2 * LM_BLOCK, TERM_BLOCK), jnp.bfloat16),
            pltpu.VMEM((units, 2 * LM_BLOCK, docs), jnp.bfloat16),
            pltpu.VMEM((units, 2 * LM_BLOCK, docs), jnp.bfloat16),
            pltpu.VMEM((nd, 8, DOC_BLOCK), jnp.float32),
            pltpu.VMEM((targets, docs), jnp.float32),
            pltpu.VMEM((land_count, targets // land_count, docs), jnp.float32),
            pltpu.VMEM((targets, docs), jnp.float32),
            pltpu.VMEM((2 * targets, docs), jnp.bfloat16),
            pltpu.VMEM((2, nz, half, 2 * targets), jnp.float32),
            pltpu.VMEM((nz, half, 2 * targets), jnp.float32),
            pltpu.VMEM((nz, half, 2 * targets), jnp.float32),
            dma((2,)), dma((3, nb)), dma((3,)), dma((nz, nb)), dma((nz, nb)), dma((nz,)), dma((nz,)),
            dma((dp_count, nb)), dma((dp_count,)),
            dma((land_count,)), dma((land_count,)), dma((land_count,)), dma((land_count,)),
            dma((nz,)), dma((nz,)), dma((nz,)), dma((nz,)),
        ],
        compiler_params=pltpu.CompilerParams(
            collective_id=0, has_side_effects=True, vmem_limit_bytes=60 * 1024 * 1024),
        cost_estimate=pl.CostEstimate(
            flops=2 * pairs * (width + 6 * targets), bytes_accessed=16 * 1024 * 1024,
            transcendentals=pairs),
    )(
        pos,
        doc_values.reshape(nd, DOC_BLOCK, width),
        land_values.reshape(nb, LM_BLOCK, width),
        coefficients.T,
    )


def solution(mesh):
    placed = (P("dp", None), P("dp", None), P(("dp", "land"), None), P(), P(("dp", "land"), None))
    return jax.shard_map(
        on_device, mesh=mesh, in_specs=placed, out_specs=P(("dp", "land"), None), check_vma=False
    )
```

time: 755 us -> 123 us (0.16)
  matrix products: 257 us -> 0 us
  local copies, waits for them, and re-layouts: 258 us -> 4.23 us
  waiting for transfers between devices: 141 us -> 0 us
  Pallas kernels: 0 us -> 118 us
  other arithmetic: 59.6 us -> 0.25 us
  blocking collectives: 19 us -> 0 us
  between operations: 13.2 us -> 0.03 us
    dot_general x68 -> x0, matrix products: 257 us -> none  [the longest x32 139 us: one_block(): jnp.einsum('dab,lbt->dlat', matches, tile_grid, preferred_element_type=jn...]
    convert_element_type x32 -> x0, local copies, waits for them, and re-layouts: 248 us -> none  [one_block(): aligned = jnp.einsum('dab,lbt->dlat', matches, tile_grid, preferred_eleme...]
    pallas_call x0 -> x1, Pallas kernels: none -> 118 us  [on_device(): pl.pallas_call(functools.partial(fused_kernel, dp_count, land_count, floa...]
    all_gather x1 -> x0, waiting for transfers between devices: 65.4 us -> none  [on_device(): land_rows = lax.all_gather(land_values, 'dp', axis=0, tiled=True)]
    psum x1 -> x0, waiting for transfers between devices: 42.8 us -> none  [on_device(): fitted = lax.psum(fitted, 'land')]
    dynamic_update_slice x32 -> x0, other arithmetic: 38.2 us -> none  [kernel_tiles(): return lax.map(one_block, (land_grid, land_ids, norm_grid))]
    reduce_scatter x1 -> x0, waiting for transfers between devices: 32.4 us -> none  [on_device(): lax.psum_scatter(summed.reshape(-1, targets), 'dp', scatter_dimension=0,...]
    all_gather x1 -> x0, blocking collectives: 19 us -> none  [on_device(): coef_rows = lax.all_gather(coefficients, 'dp', axis=0, tiled=True)]
  transfers between devices with their start and end apart: 3 -> 0, of which waited for: 3 -> 0; matrix products, arithmetic and copies ran while one was open for 0% -> 0% of each run, Pallas kernels for 0% -> 0%
where the time goes in v1:
time: 123 us
  Pallas kernels  118 us (96%)
  local copies, waits for them, and re-layouts  4.23 us (3%)
    pallas_call x1, Pallas kernels, on_device(): pl.pallas_call(functools.partial(fused_kernel, dp_count, land_count, floa...  118 us

profile of v1, /device:TPU:0, one launch (start us, length us, event | category | flops | bytes accessed | tf_op | source)
XLA Modules:
  0.0 122.7 jit_solution(10325245560496505559)
XLA Ops:
  0.0 0.8 copy.11
  0.8 0.8 copy.12
  1.6 0.1 copy.13
  1.6 0.3 select_reduce_fusion
  1.9 0.2 copy.14
  2.1 0.7 reshape.16.pos_ref
  2.8 118.2 %shard_map.55 = f32[512,64]{1,0:T(8,128)} custom-call(s32[3072]{0:T(1024)} %reshape.16.pos_ref, bf16[12,128,1024]{2,1,0:T(8,128)(2,1)} %bitcast.7, bf16[4,128,1024]{2,1,0:T(8,128)(2,1)} %bitcast.8, bf16[64,512]{1,0:T(8,128)(2,1)} %bitcast.9), custom_call_target="tpu_custom_call" | custom-call | flops 17716740096 | bytes 16777216 | tf_op jit(solution)/shard_map/pallas_call | solution.py:371
  121.0 1.7 %copy.15 = f32[512,64]{0,1:T(8,128)} copy(f32[512,64]{1,0:T(8,128)} %shard_map.55) | data formatting | bytes 262144 | tf_op jit(solution)/shard_map/pallas_call | solution.py:371
  (1 shorter events, 0.0 us)

commit v2 on v1

--- a/solution.py
+++ b/solution.py
@@ -32,6 +32,7 @@
     nz = dp_count // 2
     nb = land_ref.shape[0]
     nd = doc_ref.shape[0]
+    group = 6 if nd % 6 == 0 else 2
     docs = nd * DOC_BLOCK
     targets = coef_ref.shape[0]
     part_rows = targets // land_count
@@ -124,10 +125,10 @@
             axis=1)
         unit = q * nb + b
 
-        def doc_pair(i, carry):
+        def doc_pair(d0):
             highs, lows = [], []
             for h in range(2):
-                d = i * 2 + h
+                d = d0 + h
                 sides = []
                 for c in range(2):
                     first = (((q * 2 + c) * nb + b) * nd + d) * ACTIVE
@@ -145,15 +146,19 @@
                 lows.append((kernel - high.astype(jnp.float32)).astype(jnp.bfloat16))
             high = jnp.concatenate(highs, axis=1)
             low = jnp.concatenate(lows, axis=1)
-            cols = pl.ds(pl.multiple_of(i * 2 * DOC_BLOCK, 2 * DOC_BLOCK), 2 * DOC_BLOCK)
+            cols = pl.ds(pl.multiple_of(d0 * DOC_BLOCK, 2 * DOC_BLOCK), 2 * DOC_BLOCK)
             kh[unit, :, cols] = high
             kl[unit, :, cols] = low
             fit[:, cols] += (
                 jnp.dot(coef, high, preferred_element_type=jnp.float32)
                 + jnp.dot(coef, low, preferred_element_type=jnp.float32))
+
+        def doc_group(i, carry):
+            for pair in range(group // 2):
+                doc_pair(i * group + 2 * pair)
             return carry
 
-        lax.fori_loop(0, nd // 2, doc_pair, 0)
+        lax.fori_loop(0, nd // group, doc_group, 0)
 
     def place(r, way):
         hops = r // nb
@@ -265,22 +270,18 @@
     def back(i, carry):
         q = lax.rem(z + 1 + i, nz)
 
-        def back_unit(b, inner_carry):
+        pair = fpair[...]
+        for b in range(nb):
             unit = q * nb + b
-            pair = fpair[...]
-            dims = (((1,), (1,)), ((), ()))
-            summed = (
-                lax.dot_general(kh[unit], pair, dims, preferred_element_type=jnp.float32)
-                + lax.dot_general(kl[unit], pair, dims, preferred_element_type=jnp.float32))
+            both = lax.dot_general(
+                jnp.concatenate([kh[unit], kl[unit]], axis=0), pair, (((1,), (1,)), ((), ())),
+                preferred_element_type=jnp.float32)
+            summed = both[:2 * LM_BLOCK] + both[2 * LM_BLOCK:]
             summed = summed + pltpu.roll(summed, targets, 1)
-            at = pl.ds(pl.multiple_of(b * half, half), half)
             for c in range(2):
                 low = c * LM_BLOCK
-                sbuf[c, q, at, :] = jnp.where(
+                sbuf[c, q, b * half:(b + 1) * half, :] = jnp.where(
                     lane < targets, summed[low:low + half], summed[low + half:low + LM_BLOCK])
-            return inner_carry
-
-        lax.fori_loop(0, nb, back_unit, 0)
         mate_copy(q).start()
 
         @pl.when(i > 0)

time: 123 us -> 117 us (0.951)
  Pallas kernels: 118 us -> 112 us
    pallas_call x1, Pallas kernels: 118 us -> 112 us  [on_device(): pl.pallas_call(functools.partial(fused_kernel, dp_count, land_count, floa...]
where the time goes in v2:
time: 117 us
  Pallas kernels  112 us (96%)
  local copies, waits for them, and re-layouts  4.23 us (4%)
    pallas_call x1, Pallas kernels, on_device(): pl.pallas_call(functools.partial(fused_kernel, dp_count, land_count, floa...  112 us

profile of v2, /device:TPU:0, one launch (start us, length us, event | category | flops | bytes accessed | tf_op | source)
XLA Modules:
  0.0 116.7 jit_solution(4642037871530859378)
XLA Ops:
  0.0 0.8 copy.11
  0.8 0.8 copy.12
  1.6 0.1 copy.13
  1.6 0.3 select_reduce_fusion
  1.9 0.2 copy.14
  2.1 0.7 reshape.16.pos_ref
  2.8 112.2 %shard_map.55 = f32[512,64]{1,0:T(8,128)} custom-call(s32[3072]{0:T(1024)} %reshape.16.pos_ref, bf16[12,128,1024]{2,1,0:T(8,128)(2,1)} %bitcast.7, bf16[4,128,1024]{2,1,0:T(8,128)(2,1)} %bitcast.8, bf16[64,512]{1,0:T(8,128)(2,1)} %bitcast.9), custom_call_target="tpu_custom_call" | custom-call | flops 17716740096 | bytes 16777216 | tf_op jit(solution)/shard_map/pallas_call | solution.py:372
  115.0 1.7 %copy.15 = f32[512,64]{0,1:T(8,128)} copy(f32[512,64]{1,0:T(8,128)} %shard_map.55) | data formatting | bytes 262144 | tf_op jit(solution)/shard_map/pallas_call | solution.py:372
  (1 shorter events, 0.0 us)

commit v3 on v2

--- a/solution.py
+++ b/solution.py
@@ -32,7 +32,7 @@
     nz = dp_count // 2
     nb = land_ref.shape[0]
     nd = doc_ref.shape[0]
-    group = 6 if nd % 6 == 0 else 2
+    group = 12 if nd % 12 == 0 else 2
     docs = nd * DOC_BLOCK
     targets = coef_ref.shape[0]
     part_rows = targets // land_count
@@ -282,13 +282,13 @@
                 low = c * LM_BLOCK
                 sbuf[c, q, b * half:(b + 1) * half, :] = jnp.where(
                     lane < targets, summed[low:low + half], summed[low + half:low + LM_BLOCK])
+            if b == min(1, nb - 1):
+                @pl.when(i > 0)
+                def _():
+                    before = lax.rem(z + i, nz)
+                    finish(before)
+                    chip_copy(before, z).start()
         mate_copy(q).start()
-
-        @pl.when(i > 0)
-        def _():
-            before = lax.rem(z + i, nz)
-            finish(before)
-            chip_copy(before, z).start()
         return carry
 
     lax.fori_loop(0, nz, back, 0)

time: 117 us -> 116 us (level)
  no operation moved by 1% of the time
where the time goes in v3:
time: 116 us
  Pallas kernels  112 us (97%)
  local copies, waits for them, and re-layouts  4.23 us (4%)
    pallas_call x1, Pallas kernels, on_device(): pl.pallas_call(functools.partial(fused_kernel, dp_count, land_count, floa...  112 us

profile of v3, /device:TPU:0, one launch (start us, length us, event | category | flops | bytes accessed | tf_op | source)
XLA Modules:
  0.0 116.2 jit_solution(387832029704897157)
XLA Ops:
  0.0 0.8 copy.11
  0.8 0.8 copy.12
  1.6 0.1 copy.13
  1.6 0.3 select_reduce_fusion
  1.9 0.2 copy.14
  2.1 0.7 reshape.16.pos_ref
  2.8 111.7 %shard_map.55 = f32[512,64]{1,0:T(8,128)} custom-call(s32[3072]{0:T(1024)} %reshape.16.pos_ref, bf16[12,128,1024]{2,1,0:T(8,128)(2,1)} %bitcast.7, bf16[4,128,1024]{2,1,0:T(8,128)(2,1)} %bitcast.8, bf16[64,512]{1,0:T(8,128)(2,1)} %bitcast.9), custom_call_target="tpu_custom_call" | custom-call | flops 17716740096 | bytes 16777216 | tf_op jit(solution)/shard_map/pallas_call | solution.py:372
  114.4 1.7 %copy.15 = f32[512,64]{0,1:T(8,128)} copy(f32[512,64]{1,0:T(8,128)} %shard_map.55) | data formatting | bytes 262144 | tf_op jit(solution)/shard_map/pallas_call | solution.py:372
  (1 shorter events, 0.0 us)
